TPU v7x, 32 devices: a whole 2x2x4 slice. The times are simulated.
32 devices in a mesh: member: 2 (over x), tile: 16 (over z, y, core).
Axes of the slice: x: 2, y: 2, z: 4, core: 2. Of those that a mesh axis runs over, the one named last changes fastest.
Arguments:
- inputs: bfloat16 [2, 8192, 512], P('member', 'tile'), may hold values from -6 to 6
- noise: bfloat16 [2, 8192, 128], P('member', 'tile'), may hold values from -6 to 6
- neighbours: int32 [8, 8192], P(None, 'tile'), may hold values from 0 to 639, as said below
- region_map: int32 [16], P('tile'), may hold values from 0 to 7, as said below
- msg_weight: bfloat16 [512, 512], replicated, may hold values from -0.25 to 0.25
- up_weight: bfloat16 [512, 1024], replicated, may hold values from -0.25 to 0.25
- down_weight: bfloat16 [1024, 512], replicated, may hold values from -0.1875 to 0.1875
- student_in: bfloat16 [512, 512], replicated, may hold values from -0.25 to 0.25
- student_noise: bfloat16 [128, 512], replicated, may hold values from -0.5 to 0.5
- student_out: bfloat16 [512, 512], replicated, may hold values from -0.25 to 0.25
Outputs:
- teacher_out: bfloat16 [2, 8192, 512], P('member', 'tile')
- region_loss: float32 [8], replicated
- grad_in: float32 [512, 512], P('tile')
- grad_noise: float32 [128, 512], P('tile')
- grad_out: float32 [512, 512], P('tile')
Inputs may be any that keep to these rules, and one draw needn't show every extreme that they name: `neighbours`: each index lies within 64 of the cell's own row (its row plus 64); the first index of a tile's first cell is 0 and that of its last cell is 639. `region_map`: each region holds 2 tiles.
All inputs are finite; a program needn't handle non-finite values.
Results may differ from a plain program's by a relative error of at most 0.0039.
The roundings to bfloat16 on the way count: a program that leaves them out, or rounds other values in their place, can miss the bound.
Values may be sent and summed in bfloat16 or wider, within the bound.
A program may use at most 64 MiB of HBM per device.

v0:
```python
import math

import jax
import jax.numpy as jnp
from jax import lax
from jax.sharding import PartitionSpec as P

D = 512
HALO = 64
REGIONS = 8


def with_halo(cells, sides, width):
    for axis, dim in sides:
        count = lax.axis_size(axis)
        ends = count - 1
        head = lax.slice_in_dim(cells, 0, width, axis=dim)
        tail = lax.slice_in_dim(cells, cells.shape[dim] - width, cells.shape[dim], axis=dim)
        cells = jnp.concatenate(
            [
                lax.ppermute(tail, axis, [(i, (i + 1) % count) for i in range(ends)]),
                cells,
                lax.ppermute(head, axis, [((i + 1) % count, i) for i in range(ends)]),
            ],
            axis=dim,
        )
    return cells


def smooth(diff):
    return jnp.sqrt(diff * diff + 0.01) - 0.1


def smooth_grad(diff):
    return diff / jnp.sqrt(diff * diff + 0.01)


def silu_grad(value):
    sig = jax.nn.sigmoid(value)
    return sig * (1.0 + value * (1.0 - sig))


def on_device(
    inputs,
    noise,
    neighbours,
    region_map,
    msg_weight,
    up_weight,
    down_weight,
    student_in,
    student_noise,
    student_out,
):
    state = inputs[0]
    draws = noise[0]
    cells = state.shape[0]
    width = state.shape[1]
    members = lax.axis_size("member")
    tiles = lax.axis_size("tile")
    cells_all = cells * tiles
    extended = with_halo(state, (("tile", 0),), HALO)
    total = jnp.zeros((cells, width), jnp.float32)
    for column in range(neighbours.shape[0]):
        total = total + jnp.take(extended, neighbours[column], axis=0).astype(jnp.float32)
    gathered = (total / neighbours.shape[0]).astype(jnp.bfloat16)
    resid = state.astype(jnp.float32) + jnp.dot(
        gathered, msg_weight, preferred_element_type=jnp.float32
    )
    normed = (resid * lax.rsqrt(jnp.mean(resid * resid, axis=1, keepdims=True) + 1e-06)).astype(
        jnp.bfloat16
    )
    hidden = jax.nn.silu(jnp.dot(normed, up_weight, preferred_element_type=jnp.float32)).astype(
        jnp.bfloat16
    )
    teacher_state = (
        resid + jnp.dot(hidden, down_weight, preferred_element_type=jnp.float32)
    ).astype(jnp.bfloat16)
    preact = jnp.dot(state, student_in, preferred_element_type=jnp.float32) + jnp.dot(
        draws, student_noise, preferred_element_type=jnp.float32
    )
    shidden = jax.nn.silu(preact).astype(jnp.bfloat16)
    student = (
        state.astype(jnp.float32)
        + jnp.dot(shidden, student_out, preferred_element_type=jnp.float32)
    ).astype(jnp.bfloat16)
    block = cells // members
    scale = 1.0 / math.sqrt(cells_all)
    packed = (
        student.reshape(1, members, block, width),
        teacher_state.reshape(1, members, block, width),
    )
    own_s = lax.all_to_all(packed[0], "member", split_axis=1, concat_axis=0, tiled=True)
    own_t = lax.all_to_all(packed[1], "member", split_axis=1, concat_axis=0, tiled=True)
    s_all = own_s[:, 0].astype(jnp.float32)
    t_all = own_t[:, 0].astype(jnp.float32)

    def visit(carry, other):
        grads, losses = carry
        other_s, other_t = other
        cross = s_all - other_t[None]
        within = s_all - other_s[None]
        grads = (
            grads
            + smooth_grad(cross) / (members * members)
            - smooth_grad(within) / (members * (members - 1))
        )
        losses = losses + jnp.sum(
            smooth(cross) / (members * members) - smooth(within) / (2 * members * (members - 1)),
            axis=(0, 2),
        )
        return ((grads, losses), None)

    start = (jnp.zeros_like(s_all), jnp.zeros((s_all.shape[1],), jnp.float32))
    (grads, losses), _ = lax.scan(visit, start, (s_all, t_all))
    gsend = (grads * scale).astype(jnp.bfloat16)[:, None]
    returned = lax.all_to_all(gsend, "member", split_axis=0, concat_axis=1, tiled=True)
    returned, cell_loss = (returned, losses[None, None, :])
    gstudent = returned.reshape(cells, width)
    local_loss = jnp.sum(cell_loss)
    onehot = (region_map[0] == jnp.arange(REGIONS, dtype=jnp.int32)).astype(
        jnp.float32
    ) * local_loss
    region_loss = lax.psum(onehot, ("member", "tile")) / (cells_all // REGIONS * D)
    acc_out = jnp.dot(shidden.T, gstudent, preferred_element_type=jnp.float32)
    gpre = (
        jnp.dot(gstudent, student_out.T, preferred_element_type=jnp.float32) * silu_grad(preact)
    ).astype(jnp.bfloat16)
    acc_in = jnp.dot(state.T, gpre, preferred_element_type=jnp.float32)
    acc_noise = jnp.dot(draws.T, gpre, preferred_element_type=jnp.float32)
    shares = (
        lax.psum_scatter(acc_in, "tile", scatter_dimension=0, tiled=True),
        lax.psum_scatter(acc_noise, "tile", scatter_dimension=0, tiled=True),
        lax.psum_scatter(acc_out, "tile", scatter_dimension=0, tiled=True),
    )
    grad_in, grad_noise, grad_out = lax.psum((shares[0], shares[1], shares[2]), "member")
    return (teacher_state[None], region_loss, grad_in, grad_noise, grad_out)


def solution(mesh):
    in_specs = (
        P("member", "tile", None),
        P("member", "tile", None),
        P(None, "tile"),
        P("tile"),
        P(),
        P(),
        P(),
        P(),
        P(),
        P(),
    )
    out_specs = (P("member", "tile", None), P(), P("tile", None), P("tile", None), P("tile", None))
    return jax.shard_map(
        on_device, mesh=mesh, in_specs=in_specs, out_specs=out_specs, check_vma=False
    )
```

profile of v0, /device:TPU:0, one launch (start us, length us, event | category | flops | bytes accessed | tf_op | source)
XLA Modules:
  0.0 300.3 jit_solution(1542639055397939274)
XLA Ops:
  7.2 1.0 slice_bitcast_fusion.1
  8.2 2.4 collective-permute-start
  10.5 1.4 collective-permute-start.1
  12.0 1.6 fusion.29
  13.9 0.7 copy-done.1
  14.8 1.3 fusion.2
  16.1 3.7 %all-to-all-start.1 = ((bf16[1,2,256,512]{3,2,0,1:T(8,128)(2,1)}), bf16[1,2,256,512]{3,2,0,1:T(8,128)(2,1)S(1)}, u32[]{:S(2)}, u32[]{:S(2)}) async-start(bf16[1,2,256,512]{3,2,0,1:T(8,128)(2,1)} %bitcast.18), calls=%async_computation.1 | async-start | bytes 1048576 | tf_op jit(solution)/shard_map/all_to_all | solution.py:93
  20.2 2.0 gather_fusion.2
  22.2 2.6 gather_fusion.3
  24.8 2.6 gather_fusion.4
  27.5 2.6 gather_fusion.5
  30.1 2.6 gather_fusion.6
  32.7 2.6 gather_fusion.7
  35.3 2.6 gather_fusion
  37.9 2.6 gather_fusion.1
  40.6 4.4 %multiply_reduce_fusion = (f32[512]{0:T(512)S(1)}, f32[512,512]{1,0:T(8,128)}) fusion(bf16[512,512]{1,0:T(8,128)(2,1)} %param.18, bf16[512,512]{1,0:T(8,128)(2,1)} %gather_fusion.7, bf16[512,512]{1,0:T(8,128)(2,1)} %gather_fusion.6, bf16[512,512]{1,0:T(8,128)(2,1)} %gather_fusion.5, bf16[512,512]{1,0:T(8,128)(2,1)} %gather_fusion.4, ...), kind=kOutput, calls=%fused_computation.31 | convolution fusion | flops 276037120 | bytes 6297600 | tf_op jit(solution)/shard_map/dot_general | solution.py:67
  45.0 4.1 %fusion.1 = bf16[512,512]{1,0:T(8,128)(2,1)} fusion(f32[512,512]{1,0:T(8,128)} %get-tuple-element.145, bf16[1024,512]{1,0:T(8,128)(2,1)S(1)} %copy-done, bf16[512,1024]{1,0:T(8,128)(2,1)} %param.19, f32[512]{0:T(512)S(1)} %add_rsqrt_fusion), kind=kOutput, calls=%fused_computation.23 | convolution fusion | flops 1077411840 | bytes 3672064 | tf_op jit(solution)/shard_map/dot_general | solution.py:77
  49.1 3.5 %all-to-all-start = ((bf16[1,2,256,512]{3,2,0,1:T(8,128)(2,1)}), bf16[1,2,256,512]{3,2,0,1:T(8,128)(2,1)S(1)}, u32[]{:S(2)}, u32[]{:S(2)}) async-start(bf16[1,2,256,512]{3,2,0,1:T(8,128)(2,1)} %bitcast.14), calls=%async_computation | async-start | bytes 1048576 | tf_op jit(solution)/shard_map/all_to_all | solution.py:94
  52.8 7.4 %all-to-all-done = bf16[1,2,256,512]{3,2,0,1:T(8,128)(2,1)S(1)} async-done(((bf16[1,2,256,512]{3,2,0,1:T(8,128)(2,1)}), bf16[1,2,256,512]{3,2,0,1:T(8,128)(2,1)S(1)}, u32[]{:S(2)}, u32[]{:S(2)}) %all-to-all-start) | async-done | bytes 524320 | tf_op jit(solution)/shard_map/all_to_all | solution.py:94
  60.1 1.1 bitcast_convert_fusion.1
  61.2 8.8 %while.16 = (s32[]{:T(128)}, f32[2,256,512]{2,1,0:T(8,128)}, f32[256]{0:T(256)S(1)}, f32[2,256,512]{2,1,0:T(8,128)}, f32[2,256,512]{2,1,0:T(8,128)S(1)}, /*index=5*/s32[]{:T(128)}, s32[]{:T(128)}) while((s32[]{:T(128)}, f32[2,256,512]{2,1,0:T(8,128)}, f32[256]{0:T(256)S(1)}, f32[2,256,512]{2,1,0:T(8,128)}, ...), condition=%wide.region_3.5_spmd.clone, body=%wide.region_1.0_spmd.clone.sunk | while | flops 4980995 | bytes 6295644 | solution.py:115
  61.2 1.1 dynamic-slice_bitcast_fusion.3
  62.3 2.6 subtract_reduce_fusion.2
  65.0 1.1 dynamic-slice_bitcast_fusion.3
  66.1 3.9 %subtract_reduce_fusion.2 = (f32[256]{0:T(256)S(1)}, f32[2,256,512]{2,1,0:T(8,128)}) fusion(f32[2,256,512]{2,1,0:T(8,128)S(1)} %get-tuple-element.211, f32[256,512]{1,0:T(8,128)S(1)} %get-tuple-element.189, f32[256,512]{1,0:T(8,128)S(1)} %get-tuple-element.190, f32[2,256,512]{2,1,0:T(8,128)} %get-tuple-element.201, pred[]{:T(512)S(6)} %compare.3), kind=kLoop, calls=%fused_computation.10.clone.1 | loop fusion | flops 4980480 | bytes 4195329 | tf_op jit(solution)/shard_map/while/body/eval_jaxpr/reduce_sum | solution.py:108
  70.0 1.5 fusion.5
  71.5 10.9 %all_to_all.12 = bf16[2,1,256,512]{3,2,1,0:T(8,128)(2,1)S(1)} all-to-all(bf16[2,1,256,512]{3,2,1,0:T(8,128)(2,1)S(1)} %fusion.5), channel_id=1, replica_groups=mesh['member'=2,'tile'=16] {'member'}, dimensions={0} | all-to-all | bytes 1048576 | tf_op jit(solution)/shard_map/all_to_all | solution.py:117
  82.4 0.6 fusion.3
  83.1 0.4 copy-done.2
  83.5 0.5 convolution_bitcast_fusion
  83.9 1.3 copy.21
  85.3 1.1 copy-done.5
  86.5 1.5 fusion.34
  88.4 0.8 copy.23
  90.0 0.6 reduce_sum.32
  90.6 0.6 compare_select_fusion.8
  91.2 42.7 %psum.28 = f32[8]{0:T(128)S(1)} all-reduce(f32[8]{0:T(128)S(1)} %compare_select_fusion.8), channel_id=1, replica_groups=mesh['member'=2,'tile'=16] {'member','tile'}, use_global_device_ids=true, to_apply=%region_5.7 | all-reduce | flops 8 | bytes 64 | tf_op jit(solution)/shard_map/psum | solution.py:124
  133.9 11.2 %reduce-scatter.10.cloned.1.call-done = f32[32,512]{1,0:T(8,128)} async-done(((f32[512,512]{1,0:T(8,128)}), f32[32,512]{1,0:T(8,128)}) %reduce-scatter.10.cloned.1.call-update) | async-done | bytes 65552
  145.1 1.7 copy.22
  146.8 58.8 %reduce-scatter.8.cloned.1.call-done = f32[32,512]{1,0:T(8,128)} async-done(((f32[512,512]{1,0:T(8,128)}), f32[32,512]{1,0:T(8,128)}) %reduce-scatter.8.cloned.1.call-update) | async-done | bytes 65552 | tf_op jit(solution)/shard_map/reduce_scatter | solution.py:134
  205.6 0.5 broadcast_multiply_fusion
  206.1 57.3 %reduce-scatter.12.cloned.1.call-done = f32[8,512]{1,0:T(8,128)} async-done(((f32[128,512]{1,0:T(8,128)}), f32[8,512]{1,0:T(8,128)}) %reduce-scatter.12.cloned.1.call-update) | async-done | bytes 16400
  263.4 0.8 copy.24
  264.3 13.1 %psum.30 = f32[8,512]{0,1:T(8,128)S(1)} all-reduce(f32[8,512]{0,1:T(8,128)S(1)} %copy.24), channel_id=1, replica_groups=mesh['member'=2,'tile'=16] {'member'}, use_global_device_ids=true, to_apply=%region_9.11 | all-reduce | flops 4096 | bytes 32768 | tf_op jit(solution)/shard_map/psum | solution.py:136
  277.4 0.7 copy.20
  278.1 12.5 %all-reduce.3.cloned.1.call-done = (f32[32,512]{0,1:T(8,128)}, f32[32,512]{1,0:T(8,128)}) async-done(((f32[32,512]{0,1:T(8,128)}, f32[32,512]{1,0:T(8,128)}), (f32[32,512]{0,1:T(8,128)}, f32[32,512]{1,0:T(8,128)})) %all-reduce.3.cloned.1.call-update) | async-done | bytes 131088 | tf_op jit(solution)/shard_map/psum | solution.py:136
  290.6 1.7 copy.19
  292.3 1.5 copy.37
  (60 shorter events, 1.4 us)
Async XLA Ops:
  7.2 37.8 %copy-start = (bf16[1024,512]{1,0:T(8,128)(2,1)S(1)}, bf16[1024,512]{1,0:T(8,128)(2,1)}, u32[]{:S(2)}) copy-start(bf16[1024,512]{1,0:T(8,128)(2,1)} %param.20) | copy-start | bytes 3145732
  8.2 12.0 %collective-permute-start = (bf16[64,512]{1,0:T(8,128)(2,1)S(1)}, bf16[64,512]{1,0:T(8,128)(2,1)S(1)}, u32[]{:S(2)}, u32[]{:S(2)}) collective-permute-start(bf16[64,512]{1,0:T(8,128)(2,1)S(1)} %get-tuple-element.134), channel_id=1, source_target_pairs={{0,1},{1,2},{2,3},{3,4},{4,5},{5,6},{6,7},{7,8},{8,9},{9,10},{10,1... | collective-permute-start | bytes 196616 | tf_op jit(solution)/shard_map/ppermute | solution.py:21
  10.5 3.1 %copy-start.6 = (bf16[1,512,128]{2,1,0:T(8,128)(2,1)S(1)}, bf16[1,512,128]{2,1,0:T(8,128)(2,1)}, u32[]{:S(2)}) copy-start(bf16[1,512,128]{2,1,0:T(8,128)(2,1)} %param.15) | copy-start | bytes 393220
  10.5 3.1 %copy-start.7 = (bf16[128,512]{1,0:T(8,128)(2,1)S(1)}, bf16[128,512]{1,0:T(8,128)(2,1)}, u32[]{:S(2)}) copy-start(bf16[128,512]{1,0:T(8,128)(2,1)} %param.22) | copy-start | bytes 393220
  10.5 9.6 %collective-permute-start.1 = (bf16[64,512]{1,0:T(8,128)(2,1)S(1)}, bf16[64,512]{1,0:T(8,128)(2,1)S(1)}, u32[]{:S(2)}, u32[]{:S(2)}) collective-permute-start(bf16[64,512]{1,0:T(8,128)(2,1)S(1)} %get-tuple-element.135), channel_id=1, source_target_pairs={{1,0},{2,1},{3,2},{4,3},{5,4},{6,5},{7,6},{8,7},{9,8},{10,9},{11,1... | collective-permute-start | bytes 196616 | tf_op jit(solution)/shard_map/ppermute | solution.py:23
  13.6 1.0 copy-start.1
  13.6 1.2 copy-start.9
  14.8 1.3 copy-start.3
  16.1 3.7 %copy-start.8 = (s32[8,512]{1,0:T(8,128)S(1)}, s32[8,512]{1,0:T(8,128)}, u32[]{:S(2)}) copy-start(s32[8,512]{1,0:T(8,128)} %param.16) | copy-start | bytes 49156
  16.1 33.0 %all-to-all-start.1 = ((bf16[1,2,256,512]{3,2,0,1:T(8,128)(2,1)}), bf16[1,2,256,512]{3,2,0,1:T(8,128)(2,1)S(1)}, u32[]{:S(2)}, u32[]{:S(2)}) async-start(bf16[1,2,256,512]{3,2,0,1:T(8,128)(2,1)} %bitcast.18), calls=%async_computation.1 | async-start | bytes 1048576 | tf_op jit(solution)/shard_map/all_to_all | solution.py:93
  49.1 11.0 %all-to-all-start = ((bf16[1,2,256,512]{3,2,0,1:T(8,128)(2,1)}), bf16[1,2,256,512]{3,2,0,1:T(8,128)(2,1)S(1)}, u32[]{:S(2)}, u32[]{:S(2)}) async-start(bf16[1,2,256,512]{3,2,0,1:T(8,128)(2,1)} %bitcast.14), calls=%async_computation | async-start | bytes 1048576 | tf_op jit(solution)/shard_map/all_to_all | solution.py:94
  52.6 92.5 %reduce-scatter.10.cloned.1.call-start = ((), (), s32[]{:S(2)}) async-start(), calls=%async_computation.7 | async-start | bytes 1114112
  70.0 12.4 %copy-start.4 = (f32[512,512]{1,0:T(8,128)S(1)}, f32[512,512]{1,0:T(8,128)}, u32[]{:S(2)}) copy-start(f32[512,512]{1,0:T(8,128)} %copy-done.3) | copy-start | bytes 3145732
  70.0 12.4 %copy-start.10 = (bf16[512,512]{1,0:T(8,128)(2,1)S(1)}, bf16[512,512]{1,0:T(8,128)(2,1)}, u32[]{:S(2)}) copy-start(bf16[512,512]{1,0:T(8,128)(2,1)} %param.23) | copy-start | bytes 1572868
  82.4 1.0 copy-start.2
  85.3 1.2 copy-start.5
  85.3 120.3 %reduce-scatter.8.cloned.1.call-start = ((), (), s32[]{:S(2)}) async-start(), calls=%async_computation.6 | async-start | bytes 1114112 | tf_op jit(solution)/shard_map/reduce_scatter | solution.py:134
  88.0 175.4 %reduce-scatter.12.cloned.1.call-start = ((), (), s32[]{:S(2)}) async-start(), calls=%async_computation.8 | async-start | bytes 278528
  89.3 201.4 %all-reduce.3.cloned.1.call-start = ((), (), s32[]{:S(2)}) async-start(), calls=%async_computation.9 | async-start | bytes 655360 | tf_op jit(solution)/shard_map/psum | solution.py:136
Sparse Core Ops, SparseCore 0:
  85.4 59.6 reduce-scatter.9
  149.1 56.4 reduce-scatter.7
  209.1 54.2 reduce-scatter.11
  265.7 24.8 all-reduce.2
where the time goes:
time: 301 us; the launch traced here: 300 us
  waiting for transfers between devices  147 us (49%)
  blocking collectives  66.7 us (22%)
  local copies, waits for them, and re-layouts  34.6 us (11%)
  between operations  14.8 us (5%)
  matrix products  14.6 us (5%)
  starting transfers between devices  11.2 us (4%)
  other arithmetic  11.2 us (4%)
    unnamed x6, waiting for transfers between devices  68.5 us
    reduce_scatter x1, waiting for transfers between devices, on_device(): lax.psum_scatter(acc_out, 'tile', scatter_dimension=0, tiled=True)  58.8 us
    psum x1, blocking collectives, on_device(): lax.psum(onehot, ('member', 'tile')) / (cells_all // REGIONS * D)  42.7 us
    gather x8, local copies, waits for them, and re-layouts, on_device(): jnp.take(extended, neighbours[column], axis=0).astype(jnp.float32)  20.3 us
    psum x1, blocking collectives, on_device(): lax.psum((shares[0], shares[1], shares[2]), 'member')  13.1 us
    psum x1, waiting for transfers between devices, on_device(): lax.psum((shares[0], shares[1], shares[2]), 'member')  12.5 us
    unnamed x29, local copies, waits for them, and re-layouts  11.1 us
    all_to_all x1, blocking collectives, on_device(): lax.all_to_all(gsend, 'member', split_axis=0, concat_axis=1, tiled=True)  10.9 us
  transfers between devices with their start and end apart: 8, of which 5 were waited for; matrix products, arithmetic and copies ran while one was open for 13% of the time, Pallas kernels for 0%

commit v1 on v0

v1 whole, which is shorter than its diff:
```python
import functools
import math

import jax
import jax.numpy as jnp
from jax import lax
from jax.experimental import pallas as pl
from jax.experimental.pallas import tpu as pltpu
from jax.sharding import PartitionSpec as P

HALO = 64
REGIONS = 8
MESH = pl.DeviceIdType.MESH
F32 = jnp.float32
BF16 = jnp.bfloat16


def dot(a, b):
    return jnp.dot(a, b, preferred_element_type=F32)


def dot_tn(a, b):
    return lax.dot_general(a, b, (((0,), (0,)), ((), ())), preferred_element_type=F32)


def dot_nt(a, b):
    return lax.dot_general(a, b, (((1,), (1,)), ((), ())), preferred_element_type=F32)


def tile_digits(tiles):
    digits = []
    stride = 1
    for _ in range(2):
        if tiles // stride % 2 == 0 and tiles // stride > 2:
            digits.append((stride, 2))
            stride *= 2
    digits.append((stride, tiles // stride))
    return digits


def orders(tiles):
    digits = tile_digits(tiles)
    first = [digits[0], "member"] + digits[1:]
    second = digits[:2] + ["member"] + digits[2:]
    return first, second


def count_of(step, members):
    return members if step == "member" else step[1]


def slot_of(order, members, member, tile):
    slot = 0
    for step in order:
        n = count_of(step, members)
        slot = slot * n + (member if step == "member" else tile // step[0] % n)
    return slot


def layout(members, tiles):
    names = ["left", "right"]
    for o in range(1, members):
        names += [("state", o), ("noise", o), ("teacher", o)]
    for s, order in enumerate(orders(tiles)):
        for k, step in enumerate(order):
            for o in range(1, count_of(step, members)):
                names.append(("grad", s, k, o))
                if s == 0:
                    names.append(("loss", k, o))
        for o in range(1, members):
            names.append(("share", s, o))
    return {name: i for i, name in enumerate(names)}


def kernel(
    members,
    tiles,
    reduce_here,
    state_ref,
    noise_ref,
    neigh_ref,
    region_ref,
    msg_ref,
    up_ref,
    down_ref,
    sin_ref,
    snoise_ref,
    sout_ref,
    teacher_ref,
    loss_ref,
    gin_ref,
    gnoise_ref,
    gout_ref,
    ext,
    gathered,
    x_all,
    n_all,
    t_all,
    s_all,
    pre_all,
    sh_all,
    g_all,
    send_sem,
    recv_sem,
    *bufs,
):
    cells, width = state_ref.shape
    block = cells // members
    m = lax.axis_index("member")
    t = lax.axis_index("tile")
    ids = layout(members, tiles)
    streams = orders(tiles)

    def peer(step, o):
        if step == "member":
            other = lax.rem(m + o, members)
            return (other, t), other
        stride, n = step
        digit = lax.rem(t // stride, n)
        other = lax.rem(digit + o, n)
        return (m, t + (other - digit) * stride), other

    def digit_of(step):
        return m if step == "member" else lax.rem(t // step[0], step[1])

    def copy(name, src, dst, device):
        i = ids[name]
        return pltpu.make_async_remote_copy(
            src_ref=src,
            dst_ref=dst,
            send_sem=send_sem.at[i],
            recv_sem=recv_sem.at[i],
            device_id=device,
            device_id_type=MESH,
        )

    barrier = pltpu.get_barrier_semaphore()
    groups = ["member"] + (tile_digits(tiles) if reduce_here else [])
    waits = 0
    for step in groups:
        for o in range(1, count_of(step, members)):
            device, _ = peer(step, o)
            pl.semaphore_signal(barrier, inc=1, device_id=device, device_id_type=MESH)
            waits += 1

    @pl.when(t > 0)
    def _():
        pl.semaphore_signal(barrier, inc=1, device_id=(m, t - 1), device_id_type=MESH)

    @pl.when(t < tiles - 1)
    def _():
        pl.semaphore_signal(barrier, inc=1, device_id=(m, t + 1), device_id_type=MESH)

    ends = jnp.where(t > 0, 1, 0) + jnp.where(t < tiles - 1, 1, 0)
    pl.semaphore_wait(barrier, waits + ends)

    to_left = copy("left", state_ref.at[pl.ds(0, HALO)], ext.at[pl.ds(HALO + cells, HALO)], (m, t - 1))
    to_right = copy("right", state_ref.at[pl.ds(cells - HALO, HALO)], ext.at[pl.ds(0, HALO)], (m, t + 1))

    @pl.when(t > 0)
    def _():
        to_left.start()

    @pl.when(t < tiles - 1)
    def _():
        to_right.start()

    pending = []
    sent = {}
    for o in range(1, members):
        device, other = peer("member", o)
        rows = pl.ds(pl.multiple_of(other * block, block), block)
        slot = pl.ds(o * block, block)
        sent["state", o] = copy(("state", o), state_ref.at[rows], x_all.at[slot], device)
        sent["noise", o] = copy(("noise", o), noise_ref.at[rows], n_all.at[slot], device)
        sent["state", o].start()
        sent["noise", o].start()
        sent["teacher", o] = copy(("teacher", o), teacher_ref.at[rows], t_all.at[slot], device)

    own = pl.ds(pl.multiple_of(m * block, block), block)
    x_all[pl.ds(0, block)] = state_ref[own, :]
    n_all[pl.ds(0, block)] = noise_ref[own, :]
    ext[pl.ds(HALO, cells)] = state_ref[...]

    def student(o):
        rows = pl.ds(o * block, block)
        x = x_all[rows, :]
        pre = dot(x, sin_ref[...]) + dot(n_all[rows, :], snoise_ref[...])
        pre_all[rows, :] = pre
        sh = (pre * jax.nn.sigmoid(pre)).astype(BF16)
        sh_all[rows, :] = sh
        s_all[rows, :] = (x.astype(F32) + dot(sh, sout_ref[...])).astype(BF16)

    student(0)

    zeros = jnp.zeros((HALO, width), BF16)

    @pl.when(t > 0)
    def _():
        to_right.wait_recv()

    @pl.when(t == 0)
    def _():
        ext[pl.ds(0, HALO)] = zeros

    @pl.when(t < tiles - 1)
    def _():
        to_left.wait_recv()

    @pl.when(t == tiles - 1)
    def _():
        ext[pl.ds(HALO + cells, HALO)] = zeros

    span = 128
    reach = span + 2 * HALO
    nbrs = neigh_ref.shape[0]
    for b in range(cells // span):
        lines = lax.broadcasted_iota(jnp.int32, (reach, span), 0) + b * span
        times = jnp.zeros((reach, span), F32)
        for k in range(nbrs):
            index = neigh_ref[pl.ds(k, 1), pl.ds(b * span, span)]
            times = times + jnp.where(lines == index, 1.0, 0.0)
        total = dot_tn(times.astype(BF16), ext[pl.ds(b * span, reach), :])
        gathered[pl.ds(b * span, span)] = (total / nbrs).astype(BF16)

    def teacher(rows):
        resid = state_ref[rows, :].astype(F32) + dot(gathered[rows, :], msg_ref[...])
        mean = jnp.mean(resid * resid, axis=1, keepdims=True)
        normed = (resid * lax.rsqrt(mean + 1e-06)).astype(BF16)
        up = dot(normed, up_ref[...])
        hidden = (up * jax.nn.sigmoid(up)).astype(BF16)
        out = (resid + dot(hidden, down_ref[...])).astype(BF16)
        teacher_ref[rows, :] = out
        return out

    for o in range(1, members):
        _, other = peer("member", o)
        teacher(pl.ds(pl.multiple_of(other * block, block), block))
        sent["teacher", o].start()
    t_all[pl.ds(0, block)] = teacher(own)

    for o in range(1, members):
        sent["state", o].wait_recv()
        sent["noise", o].wait_recv()
        student(o)
    for o in range(1, members):
        sent["teacher", o].wait_recv()

    chunk = 16
    scale = 1.0 / math.sqrt(cells * tiles)
    c_cross = 1.0 / (members * members)
    c_within = 1.0 / (members * (members - 1))

    def visit(i, losses):
        base = pl.multiple_of(i * chunk, chunk)
        rows = [pl.ds(pl.multiple_of(j * block + base, chunk), chunk) for j in range(members)]
        st = [s_all[r, :].astype(F32) for r in rows]
        te = [t_all[r, :].astype(F32) for r in rows]
        grads = [jnp.zeros((chunk, width), F32) for _ in rows]
        cross = jnp.zeros((chunk, width), F32)
        within = jnp.zeros((chunk, width), F32)
        for a in range(members):
            for b in range(members):
                d = st[a] - te[b]
                q = d * d + 0.01
                inv = lax.rsqrt(q)
                grads[a] = grads[a] + d * inv
                cross = cross + (q * inv - 0.1)
        grads = [g * c_cross for g in grads]
        for a in range(members):
            for b in range(a + 1, members):
                d = st[a] - st[b]
                q = d * d + 0.01
                inv = lax.rsqrt(q)
                slope = d * inv * c_within
                grads[a] = grads[a] - slope
                grads[b] = grads[b] + slope
                within = within + (q * inv - 0.1)
        for r, g in zip(rows, grads):
            g_all[r, :] = (g * scale).astype(BF16)
        return losses + (cross * c_cross - within * c_within)

    losses = lax.fori_loop(0, block // chunk, visit, jnp.zeros((chunk, width), F32))
    total = jnp.sum(losses, keepdims=True)
    lane = lax.broadcasted_iota(jnp.int32, (8, 128), 1)
    onehot = jnp.where(lane == region_ref[0], 1.0, 0.0) * total

    sig = jax.nn.sigmoid(pre_all[...])
    if not reduce_here:
        loss_ref[...] = onehot
        g = g_all[...]
        gout_ref[...] = dot_tn(sh_all[...], g)
        pre = pre_all[...]
        slope = sig * (1.0 + pre * (1.0 - sig))
        gpre = (dot_nt(g, sout_ref[...]) * slope).astype(BF16)
        gin_ref[...] = dot_tn(x_all[...], gpre)
        gnoise_ref[...] = dot_tn(n_all[...], gpre)
        for o in range(1, members):
            for what in ("state", "noise", "teacher"):
                sent[what, o].wait_send()
    else:
        bufs = list(bufs)
        loss_bufs = [bufs.pop(0) for _ in streams[0]]
        wire, part, land, share = [], [], [], []
        for order in streams:
            wire.append([bufs.pop(0) for _ in order])
            part.append([bufs.pop(0) for _ in order])
            land.append([bufs.pop(0) for _ in order])
            final = bufs.pop(0)
            share.append((final, bufs.pop(0)))
        column = width // members
        loss_now = [onehot]

        def start(s, k):
            step = streams[s][k]
            n = count_of(step, members)
            size = wire[s][k].shape[0] // n
            for o in range(1, n):
                device, other = peer(step, o)
                c = copy(
                    ("grad", s, k, o),
                    wire[s][k].at[pl.ds(other * size, size)],
                    land[s][k].at[o - 1],
                    device,
                )
                c.start()
                sent["grad", s, k, o] = c

        def finish(s, k):
            step = streams[s][k]
            n = count_of(step, members)
            size = wire[s][k].shape[0] // n
            mine = digit_of(step) * size
            for o in range(1, n):
                sent["grad", s, k, o].wait_recv()
            for i in range(size):
                value = part[s][k][mine + i]
                for o in range(1, n):
                    value = value + land[s][k][o - 1, i].astype(F32)
                if k + 1 < len(streams[s]):
                    part[s][k + 1][i] = value
                    wire[s][k + 1][i] = value.astype(BF16)
                else:
                    share[s][0][...] = value.astype(BF16)

        def start_loss(k):
            step = streams[0][k]
            mine = digit_of(step)
            loss_bufs[k][mine] = loss_now[0]
            for o in range(1, count_of(step, members)):
                device, _ = peer(step, o)
                c = copy(("loss", k, o), loss_bufs[k].at[mine], loss_bufs[k].at[mine], device)
                c.start()
                sent["loss", k, o] = c

        def finish_loss(k):
            n = count_of(streams[0][k], members)
            for o in range(1, n):
                sent["loss", k, o].wait_recv()
            value = loss_bufs[k][0]
            for j in range(1, n):
                value = value + loss_bufs[k][j]
            loss_now[0] = value

        def put(s, row, acc, member):
            rows = acc.shape[0] // tiles
            for j in range(tiles):
                slot = slot_of(streams[s], members, member, j)
                value = acc[j * rows : (j + 1) * rows]
                part[s][0][slot, row : row + rows] = value
                if rows % 16:
                    value = jnp.concatenate([value, jnp.zeros((-rows % 16, column), F32)])
                wire[s][0][slot, row : row + value.shape[0]] = value.astype(BF16)

        start_loss(0)
        for j in range(members):
            cols = pl.ds(j * column, column)
            put(0, 0, dot_tn(sh_all[...], g_all[:, cols]), j)
        start(0, 0)
        pre = pre_all[...]
        slope = sig * (1.0 + pre * (1.0 - sig))
        sh_all[...] = (dot_nt(g_all[...], sout_ref[...]) * slope).astype(BF16)
        rows_in = width // tiles
        for j in range(members):
            cols = pl.ds(j * column, column)
            put(1, 0, dot_tn(x_all[...], sh_all[:, cols]), j)
            put(1, rows_in, dot_tn(n_all[...], sh_all[:, cols]), j)
        start(1, 0)
        last = len(streams[0])
        for k in range(last):
            finish_loss(k)
            if k + 1 < last:
                start_loss(k + 1)
            for s in range(2):
                finish(s, k)
                if k + 1 < last:
                    start(s, k + 1)
                else:
                    for o in range(1, members):
                        device, _ = peer("member", o)
                        c = copy(("share", s, o), share[s][0], share[s][1].at[o - 1], device)
                        c.start()
                        sent["share", s, o] = c
        loss_ref[...] = loss_now[0] * (1.0 / (cells * tiles // REGIONS * width))

        def emit(s, value, member):
            cols = pl.ds(pl.multiple_of(member * column, column), column)
            if s == 0:
                gout_ref[:, cols] = value
            else:
                gin_ref[:, cols] = value[:rows_in]
                gnoise_ref[:, cols] = value[rows_in : rows_in + gnoise_ref.shape[0]]

        for s in range(2):
            emit(s, share[s][0][...].astype(F32), m)
            for o in range(1, members):
                sent["share", s, o].wait_recv()
                emit(s, share[s][1][o - 1].astype(F32), lax.rem(m + members - o, members))
        for c in sent.values():
            c.wait_send()

    @pl.when(t > 0)
    def _():
        to_left.wait_send()

    @pl.when(t < tiles - 1)
    def _():
        to_right.wait_send()


def on_device(members, tiles, *args):
    state, noise, neighbours, region_map = args[0][0], args[1][0], args[2], args[3]
    weights = args[4:]
    cells, width = state.shape
    draws = noise.shape[1]
    hidden = weights[3].shape[1]
    rows = [hidden // tiles, width // tiles, draws // tiles]
    column = width // members
    reduce_here = (
        rows[0] % 16 == 0
        and rows[1] % 16 == 0
        and rows[2] % 8 == 0
        and column % 128 == 0
        and hidden == width
        and tiles >= 8
        and members > 1
    )
    scratch = [
        pltpu.VMEM((cells + 2 * HALO, width), BF16),
        pltpu.VMEM((cells, width), BF16),
        pltpu.VMEM((cells, width), BF16),
        pltpu.VMEM((cells, draws), BF16),
        pltpu.VMEM((cells, width), BF16),
        pltpu.VMEM((cells, width), BF16),
        pltpu.VMEM((cells, hidden), F32),
        pltpu.VMEM((cells, hidden), BF16),
        pltpu.VMEM((cells, width), BF16),
        pltpu.SemaphoreType.DMA((len(layout(members, tiles)),)),
        pltpu.SemaphoreType.DMA((len(layout(members, tiles)),)),
    ]
    if reduce_here:
        shapes = ((rows[1], width), (rows[2], width), (rows[0], width))
        streams = orders(tiles)
        for step in streams[0]:
            scratch.append(pltpu.VMEM((count_of(step, members), 8, 128), F32))
        high = [rows[0], rows[1] + -(-rows[2] // 16) * 16]
        for order, tall in zip(streams, high):
            sizes = []
            left = members * tiles
            for step in order:
                sizes.append((left, count_of(step, members)))
                left //= count_of(step, members)
            scratch += [pltpu.VMEM((size, tall, column), BF16) for size, _ in sizes]
            scratch += [pltpu.VMEM((size, tall, column), F32) for size, _ in sizes]
            scratch += [pltpu.VMEM((n - 1, size // n, tall, column), BF16) for size, n in sizes]
            scratch.append(pltpu.VMEM((tall, column), BF16))
            scratch.append(pltpu.VMEM((members - 1, tall, column), BF16))
    else:
        shapes = ((width, hidden), (draws, hidden), (hidden, width))
    vmem = pl.BlockSpec(memory_space=pltpu.VMEM)
    teacher, loss, gin, gnoise, gout = pl.pallas_call(
        functools.partial(kernel, members, tiles, reduce_here),
        out_shape=[jax.ShapeDtypeStruct((cells, width), BF16), jax.ShapeDtypeStruct((8, 128), F32)]
        + [jax.ShapeDtypeStruct(s, F32) for s in shapes],
        in_specs=[vmem] * 3 + [pl.BlockSpec(memory_space=pltpu.SMEM)] + [vmem] * 6,
        out_specs=[vmem] * 5,
        scratch_shapes=scratch,
        compiler_params=pltpu.CompilerParams(
            collective_id=0, has_side_effects=True, vmem_limit_bytes=56 * 1024 * 1024
        ),
    )(state, noise, neighbours, region_map, *weights)
    region_loss = loss[0, :REGIONS]
    if not reduce_here:
        region_loss = lax.psum(region_loss, ("member", "tile")) / (cells * tiles // REGIONS * width)
        gin, gnoise, gout = lax.psum(
            tuple(
                lax.psum_scatter(g, "tile", scatter_dimension=0, tiled=True)
                for g in (gin, gnoise, gout)
            ),
            "member",
        )
    return teacher[None], region_loss, gin, gnoise, gout


def solution(mesh):
    in_specs = (
        P("member", "tile", None),
        P("member", "tile", None),
        P(None, "tile"),
        P("tile"),
        P(),
        P(),
        P(),
        P(),
        P(),
        P(),
    )
    out_specs = (P("member", "tile", None), P(), P("tile", None), P("tile", None), P("tile", None))
    return jax.shard_map(
        functools.partial(on_device, mesh.shape["member"], mesh.shape["tile"]),
        mesh=mesh,
        in_specs=in_specs,
        out_specs=out_specs,
        check_vma=False,
    )
```

time: 301 us -> 51 us (0.17)
  waiting for transfers between devices: 147 us -> 0 us
  blocking collectives: 66.7 us -> 0 us
  Pallas kernels: 0 us -> 44.4 us
  local copies, waits for them, and re-layouts: 34.6 us -> 5.05 us
  matrix products: 14.6 us -> 0 us
  between operations: 14.8 us -> 1.29 us
  other arithmetic: 11.2 us -> 0 us
  starting transfers between devices: 11.2 us -> 0 us
    unnamed x6 -> x0, waiting for transfers between devices: 68.5 us -> none
    reduce_scatter x1 -> x0, waiting for transfers between devices: 58.8 us -> none  [on_device(): lax.psum_scatter(acc_out, 'tile', scatter_dimension=0, tiled=True)]
    psum x2 -> x0, blocking collectives: 55.8 us -> none  [the longest x1 42.7 us: on_device(): lax.psum(onehot, ('member', 'tile')) / (cells_all // REGIONS * D)]
    pallas_call x0 -> x1, Pallas kernels: none -> 44.4 us  [on_device(): pl.pallas_call(functools.partial(kernel, members, tiles, reduce_here), ou...]
    gather x8 -> x0, local copies, waits for them, and re-layouts: 20.3 us -> none  [on_device(): jnp.take(extended, neighbours[column], axis=0).astype(jnp.float32)]
    dot_general x9 -> x0, matrix products: 14.6 us -> none  [the longest x1 4.42 us: on_device(): jnp.dot(gathered, msg_weight, preferred_element_type=jnp.float32)]
    psum x1 -> x0, waiting for transfers between devices: 12.5 us -> none  [on_device(): lax.psum((shares[0], shares[1], shares[2]), 'member')]
    all_to_all x1 -> x0, blocking collectives: 10.9 us -> none  [on_device(): lax.all_to_all(gsend, 'member', split_axis=0, concat_axis=1, tiled=True)]
  transfers between devices with their start and end apart: 8 -> 0, of which waited for: 5 -> 0; matrix products, arithmetic and copies ran while one was open for 13% -> 0% of each run, Pallas kernels for 0% -> 0%
where the time goes in v1:
time: 51 us; the launch traced here: 50.7 us
  Pallas kernels  44.4 us (87%)
  local copies, waits for them, and re-layouts  5.05 us (10%)
  between operations  1.29 us (3%)
    pallas_call x1, Pallas kernels, on_device(): pl.pallas_call(functools.partial(kernel, members, tiles, reduce_here), ou...  44.4 us
    unnamed x10, local copies, waits for them, and re-layouts  3.86 us
    squeeze x1, local copies, waits for them, and re-layouts, on_device(): region_loss = loss[0, :REGIONS]  1.2 us

profile of v1, /device:TPU:0, one launch (start us, length us, event | category | flops | bytes accessed | tf_op | source)
XLA Modules:
  0.0 50.7 jit_solution(15866542250350101906)
XLA Ops:
  1.3 44.4 %shard_map.137 = (bf16[512,512]{1,0:T(8,128)(2,1)}, f32[8,128]{1,0:T(8,128)}, f32[32,512]{1,0:T(8,128)}, f32[8,512]{1,0:T(8,128)}, f32[32,512]{1,0:T(8,128)}) custom-call(bf16[512,512]{1,0:T(8,128)(2,1)} %bitcast.5, bf16[512,128]{1,0:T(8,128)(2,1)} %bitcast.7, s32[8,512]{1,0:T(8,128)} %neigh_ref.1, s32[1]{0:T(128)S(6)} %copy.19.region_ref, ...), custom_call_target="tpu_custom_call" | custom-call | tf_op jit(solution)/shard_map/pallas_call | solution.py:481
  45.6 1.2 %slice_bitcast_fusion = f32[8]{0:T(128)} fusion(f32[8,128]{1,0:T(8,128)} %get-tuple-element.11), kind=kLoop, calls=%fused_computation | loop fusion | bytes 64 | tf_op jit(solution)/shard_map/squeeze | solution.py:492
  46.8 0.0 copy-start.1
  46.8 1.9 %copy.20 = bf16[1,512,512]{2,1,0:T(8,128)(2,1)} copy(bf16[1,512,512]{2,1,0:T(8,128)(2,1)} %bitcast.6) | data formatting | bytes 1048576
  48.7 0.0 copy-done.1
  48.7 0.0 copy-start.2
  48.7 0.0 copy-start
  48.7 0.6 %copy.21 = f32[32,512]{1,0:T(8,128)} copy(f32[32,512]{1,0:T(8,128)S(1)} %copy-done.1) | data formatting | bytes 131072
  49.4 0.1 copy-done.2
  49.5 0.6 %copy.22 = f32[8,512]{1,0:T(8,128)} copy(f32[8,512]{1,0:T(8,128)S(1)} %copy-done.2) | data formatting | bytes 32768
  50.1 0.0 copy-done
  50.1 0.6 %copy.23 = f32[32,512]{1,0:T(8,128)} copy(f32[32,512]{1,0:T(8,128)S(1)} %copy-done) | data formatting | bytes 131072
Async XLA Ops:
  46.8 1.9 %copy-start.1 = (f32[32,512]{1,0:T(8,128)S(1)}, f32[32,512]{1,0:T(8,128)}, u32[]{:S(2)}) copy-start(f32[32,512]{1,0:T(8,128)} %get-tuple-element.22) | copy-start | bytes 196612
  48.7 0.7 %copy-start.2 = (f32[8,512]{1,0:T(8,128)S(1)}, f32[8,512]{1,0:T(8,128)}, u32[]{:S(2)}) copy-start(f32[8,512]{1,0:T(8,128)} %get-tuple-element.23) | copy-start | bytes 49156
  48.7 1.3 %copy-start = (f32[32,512]{1,0:T(8,128)S(1)}, f32[32,512]{1,0:T(8,128)}, u32[]{:S(2)}) copy-start(f32[32,512]{1,0:T(8,128)} %get-tuple-element.24) | copy-start | bytes 196612

commit v2 on v1

--- a/solution.py
+++ b/solution.py
@@ -42,7 +42,8 @@
     digits = tile_digits(tiles)
     first = [digits[0], "member"] + digits[1:]
     second = digits[:2] + ["member"] + digits[2:]
-    return first, second
+    third = digits[:1] + digits[2:] + ["member"] + digits[1:2]
+    return first, second, third
 
 
 def count_of(step, members):
@@ -57,10 +58,14 @@
     return slot
 
 
-def layout(members, tiles):
+def parts_of(block):
+    return 2 if block % 32 == 0 else 1
+
+
+def layout(members, tiles, parts):
     names = ["left", "right"]
     for o in range(1, members):
-        names += [("state", o), ("noise", o), ("teacher", o)]
+        names += [("state", o), ("noise", o)] + [("teacher", o, c) for c in range(parts)]
     for s, order in enumerate(orders(tiles)):
         for k, step in enumerate(order):
             for o in range(1, count_of(step, members)):
@@ -80,12 +85,12 @@
     noise_ref,
     neigh_ref,
     region_ref,
-    msg_ref,
-    up_ref,
-    down_ref,
-    sin_ref,
-    snoise_ref,
-    sout_ref,
+    msg_hbm,
+    up_hbm,
+    down_hbm,
+    sin_hbm,
+    snoise_hbm,
+    sout_hbm,
     teacher_ref,
     loss_ref,
     gin_ref,
@@ -97,9 +102,17 @@
     n_all,
     t_all,
     s_all,
-    pre_all,
+    slope_all,
     sh_all,
     g_all,
+    gpre_all,
+    msg_ref,
+    up_ref,
+    down_ref,
+    sin_ref,
+    snoise_ref,
+    sout_ref,
+    load_sem,
     send_sem,
     recv_sem,
     *bufs,
@@ -108,7 +121,9 @@
     block = cells // members
     m = lax.axis_index("member")
     t = lax.axis_index("tile")
-    ids = layout(members, tiles)
+    parts = parts_of(block)
+    part_rows = block // parts
+    ids = layout(members, tiles, parts)
     streams = orders(tiles)
 
     def peer(step, o):
@@ -134,6 +149,18 @@
             device_id_type=MESH,
         )
 
+    pairs = [
+        (sin_hbm, sin_ref),
+        (snoise_hbm, snoise_ref),
+        (sout_hbm, sout_ref),
+        (msg_hbm, msg_ref),
+        (up_hbm, up_ref),
+        (down_hbm, down_ref),
+    ]
+    loads = [pltpu.make_async_copy(a, b, load_sem.at[i]) for i, (a, b) in enumerate(pairs)]
+    for load in loads:
+        load.start()
+
     barrier = pltpu.get_barrier_semaphore()
     groups = ["member"] + (tile_digits(tiles) if reduce_here else [])
     waits = 0
@@ -175,7 +202,11 @@
         sent["noise", o] = copy(("noise", o), noise_ref.at[rows], n_all.at[slot], device)
         sent["state", o].start()
         sent["noise", o].start()
-        sent["teacher", o] = copy(("teacher", o), teacher_ref.at[rows], t_all.at[slot], device)
+        for c in range(parts):
+            rows = pl.ds(pl.multiple_of(other * block + c * part_rows, part_rows), part_rows)
+            slot = pl.ds(o * block + c * part_rows, part_rows)
+            name = ("teacher", o, c)
+            sent[name] = copy(name, teacher_ref.at[rows], t_all.at[slot], device)
 
     own = pl.ds(pl.multiple_of(m * block, block), block)
     x_all[pl.ds(0, block)] = state_ref[own, :]
@@ -186,11 +217,14 @@
         rows = pl.ds(o * block, block)
         x = x_all[rows, :]
         pre = dot(x, sin_ref[...]) + dot(n_all[rows, :], snoise_ref[...])
-        pre_all[rows, :] = pre
-        sh = (pre * jax.nn.sigmoid(pre)).astype(BF16)
+        sig = jax.nn.sigmoid(pre)
+        slope_all[rows, :] = sig * (1.0 + pre * (1.0 - sig))
+        sh = (pre * sig).astype(BF16)
         sh_all[rows, :] = sh
         s_all[rows, :] = (x.astype(F32) + dot(sh, sout_ref[...])).astype(BF16)
 
+    for load in loads[:3]:
+        load.wait()
     student(0)
 
     zeros = jnp.zeros((HALO, width), BF16)
@@ -233,19 +267,19 @@
         teacher_ref[rows, :] = out
         return out
 
+    for load in loads[3:]:
+        load.wait()
     for o in range(1, members):
         _, other = peer("member", o)
         teacher(pl.ds(pl.multiple_of(other * block, block), block))
-        sent["teacher", o].start()
+        for c in range(parts):
+            sent["teacher", o, c].start()
     t_all[pl.ds(0, block)] = teacher(own)
 
     for o in range(1, members):
         sent["state", o].wait_recv()
         sent["noise", o].wait_recv()
         student(o)
-    for o in range(1, members):
-        sent["teacher", o].wait_recv()
-
     chunk = 16
     scale = 1.0 / math.sqrt(cells * tiles)
     c_cross = 1.0 / (members * members)
@@ -280,24 +314,31 @@
             g_all[r, :] = (g * scale).astype(BF16)
         return losses + (cross * c_cross - within * c_within)
 
-    losses = lax.fori_loop(0, block // chunk, visit, jnp.zeros((chunk, width), F32))
+    def backward(c):
+        for j in range(members):
+            rows = pl.ds(j * block + c * part_rows, part_rows)
+            gpre_all[rows, :] = (dot_nt(g_all[rows, :], sout_ref[...]) * slope_all[rows, :]).astype(BF16)
+
+    losses = jnp.zeros((chunk, width), F32)
+    steps = part_rows // chunk
+    for c in range(parts):
+        for o in range(1, members):
+            sent["teacher", o, c].wait_recv()
+        losses = lax.fori_loop(c * steps, (c + 1) * steps, visit, losses)
+        if c + 1 < parts:
+            backward(c)
     total = jnp.sum(losses, keepdims=True)
     lane = lax.broadcasted_iota(jnp.int32, (8, 128), 1)
     onehot = jnp.where(lane == region_ref[0], 1.0, 0.0) * total
 
-    sig = jax.nn.sigmoid(pre_all[...])
     if not reduce_here:
         loss_ref[...] = onehot
-        g = g_all[...]
-        gout_ref[...] = dot_tn(sh_all[...], g)
-        pre = pre_all[...]
-        slope = sig * (1.0 + pre * (1.0 - sig))
-        gpre = (dot_nt(g, sout_ref[...]) * slope).astype(BF16)
-        gin_ref[...] = dot_tn(x_all[...], gpre)
-        gnoise_ref[...] = dot_tn(n_all[...], gpre)
-        for o in range(1, members):
-            for what in ("state", "noise", "teacher"):
-                sent[what, o].wait_send()
+        gout_ref[...] = dot_tn(sh_all[...], g_all[...])
+        backward(parts - 1)
+        gin_ref[...] = dot_tn(x_all[...], gpre_all[...])
+        gnoise_ref[...] = dot_tn(n_all[...], gpre_all[...])
+        for c in sent.values():
+            c.wait_send()
     else:
         bufs = list(bufs)
         loss_bufs = [bufs.pop(0) for _ in streams[0]]
@@ -362,36 +403,31 @@
                 value = value + loss_bufs[k][j]
             loss_now[0] = value
 
-        def put(s, row, acc, member):
+        def put(s, acc):
             rows = acc.shape[0] // tiles
-            for j in range(tiles):
-                slot = slot_of(streams[s], members, member, j)
-                value = acc[j * rows : (j + 1) * rows]
-                part[s][0][slot, row : row + rows] = value
-                if rows % 16:
-                    value = jnp.concatenate([value, jnp.zeros((-rows % 16, column), F32)])
-                wire[s][0][slot, row : row + value.shape[0]] = value.astype(BF16)
+            for i in range(members):
+                for j in range(tiles):
+                    slot = slot_of(streams[s], members, i, j)
+                    value = acc[j * rows : (j + 1) * rows, i * column : (i + 1) * column]
+                    if rows % 16:
+                        value = jnp.concatenate([value, jnp.zeros((-rows % 16, column), F32)])
+                    part[s][0][slot] = value
+                    wire[s][0][slot] = value.astype(BF16)
 
         start_loss(0)
-        for j in range(members):
-            cols = pl.ds(j * column, column)
-            put(0, 0, dot_tn(sh_all[...], g_all[:, cols]), j)
+        put(0, dot_tn(sh_all[...], g_all[...]))
         start(0, 0)
-        pre = pre_all[...]
-        slope = sig * (1.0 + pre * (1.0 - sig))
-        sh_all[...] = (dot_nt(g_all[...], sout_ref[...]) * slope).astype(BF16)
-        rows_in = width // tiles
-        for j in range(members):
-            cols = pl.ds(j * column, column)
-            put(1, 0, dot_tn(x_all[...], sh_all[:, cols]), j)
-            put(1, rows_in, dot_tn(n_all[...], sh_all[:, cols]), j)
+        backward(parts - 1)
+        put(1, dot_tn(x_all[...], gpre_all[...]))
         start(1, 0)
+        put(2, dot_tn(n_all[...], gpre_all[...]))
+        start(2, 0)
         last = len(streams[0])
         for k in range(last):
             finish_loss(k)
             if k + 1 < last:
                 start_loss(k + 1)
-            for s in range(2):
+            for s in range(len(streams)):
                 finish(s, k)
                 if k + 1 < last:
                     start(s, k + 1)
@@ -405,13 +441,10 @@
 
         def emit(s, value, member):
             cols = pl.ds(pl.multiple_of(member * column, column), column)
-            if s == 0:
-                gout_ref[:, cols] = value
-            else:
-                gin_ref[:, cols] = value[:rows_in]
-                gnoise_ref[:, cols] = value[rows_in : rows_in + gnoise_ref.shape[0]]
-
-        for s in range(2):
+            out = (gout_ref, gin_ref, gnoise_ref)[s]
+            out[:, cols] = value[: out.shape[0]]
+
+        for s in range(len(streams)):
             emit(s, share[s][0][...].astype(F32), m)
             for o in range(1, members):
                 sent["share", s, o].wait_recv()
@@ -426,6 +459,16 @@
     @pl.when(t < tiles - 1)
     def _():
         to_right.wait_send()
+
+
+def hand_on(*refs):
+    loss_ref, region_ref, sem = refs[4], refs[9], refs[10]
+    copies = [pltpu.make_async_copy(refs[i], refs[5 + i], sem.at[i]) for i in range(4)]
+    for c in copies:
+        c.start()
+    region_ref[...] = loss_ref[0, : region_ref.shape[0]]
+    for c in copies:
+        c.wait()
 
 
 def on_device(members, tiles, *args):
@@ -455,15 +498,17 @@
         pltpu.VMEM((cells, hidden), F32),
         pltpu.VMEM((cells, hidden), BF16),
         pltpu.VMEM((cells, width), BF16),
-        pltpu.SemaphoreType.DMA((len(layout(members, tiles)),)),
-        pltpu.SemaphoreType.DMA((len(layout(members, tiles)),)),
+        pltpu.VMEM((cells, hidden), BF16),
     ]
+    scratch += [pltpu.VMEM(w.shape, w.dtype) for w in weights]
+    copies = len(layout(members, tiles, parts_of(cells // members)))
+    scratch += [pltpu.SemaphoreType.DMA((n,)) for n in (len(weights), copies, copies)]
     if reduce_here:
         shapes = ((rows[1], width), (rows[2], width), (rows[0], width))
         streams = orders(tiles)
         for step in streams[0]:
             scratch.append(pltpu.VMEM((count_of(step, members), 8, 128), F32))
-        high = [rows[0], rows[1] + -(-rows[2] // 16) * 16]
+        high = [rows[0], rows[1], -(-rows[2] // 16) * 16]
         for order, tall in zip(streams, high):
             sizes = []
             left = members * tiles
@@ -482,15 +527,27 @@
         functools.partial(kernel, members, tiles, reduce_here),
         out_shape=[jax.ShapeDtypeStruct((cells, width), BF16), jax.ShapeDtypeStruct((8, 128), F32)]
         + [jax.ShapeDtypeStruct(s, F32) for s in shapes],
-        in_specs=[vmem] * 3 + [pl.BlockSpec(memory_space=pltpu.SMEM)] + [vmem] * 6,
+        in_specs=[vmem] * 3 + [pl.BlockSpec(memory_space=pltpu.SMEM)]
+        + [pl.BlockSpec(memory_space=pl.ANY)] * 6,
         out_specs=[vmem] * 5,
         scratch_shapes=scratch,
         compiler_params=pltpu.CompilerParams(
             collective_id=0, has_side_effects=True, vmem_limit_bytes=56 * 1024 * 1024
         ),
     )(state, noise, neighbours, region_map, *weights)
-    region_loss = loss[0, :REGIONS]
-    if not reduce_here:
+    if reduce_here:
+        hbm = pl.BlockSpec(memory_space=pl.ANY)
+        big = (teacher, gin, gnoise, gout)
+        teacher, gin, gnoise, gout, region_loss = pl.pallas_call(
+            hand_on,
+            out_shape=[jax.ShapeDtypeStruct(a.shape, a.dtype) for a in big]
+            + [jax.ShapeDtypeStruct((REGIONS,), F32)],
+            in_specs=[hbm] * 4 + [vmem],
+            out_specs=[hbm] * 4 + [vmem],
+            scratch_shapes=[pltpu.SemaphoreType.DMA((4,))],
+        )(*big, loss)
+    else:
+        region_loss = loss[0, :REGIONS]
         region_loss = lax.psum(region_loss, ("member", "tile")) / (cells * tiles // REGIONS * width)
         gin, gnoise, gout = lax.psum(
             tuple(

time: 51 us -> 64.4 us (1.26)
  Pallas kernels: 44.4 us -> 63 us
  local copies, waits for them, and re-layouts: 5.05 us -> 0 us
    pallas_call x0 -> x1, Pallas kernels: none -> 22.7 us  [on_device(): pl.pallas_call(hand_on, out_shape=[jax.ShapeDtypeStruct(a.shape, a.dtype)...]
    pallas_call x1, Pallas kernels: 44.4 us -> 40.3 us  [on_device(): pl.pallas_call(functools.partial(kernel, members, tiles, reduce_here), ou...]
    unnamed x10 -> x0, local copies, waits for them, and re-layouts: 3.86 us -> none
    squeeze x1 -> x0, local copies, waits for them, and re-layouts: 1.2 us -> none  [on_device(): region_loss = loss[0, :REGIONS]]
where the time goes in v2:
time: 64.4 us; the launch traced here: 64.2 us
  Pallas kernels  63 us (98%)
  between operations  1.29 us (2%)
    pallas_call x1, Pallas kernels, on_device(): pl.pallas_call(functools.partial(kernel, members, tiles, reduce_here), ou...  40.3 us
    pallas_call x1, Pallas kernels, on_device(): pl.pallas_call(hand_on, out_shape=[jax.ShapeDtypeStruct(a.shape, a.dtype)...  22.7 us

profile of v2, /device:TPU:0, one launch (start us, length us, event | category | flops | bytes accessed | tf_op | source)
XLA Modules:
  0.0 64.2 jit_solution(17602744913178762554)
XLA Ops:
  1.3 40.3 %shard_map.137 = (bf16[512,512]{1,0:T(8,128)(2,1)}, f32[8,128]{1,0:T(8,128)}, f32[32,512]{1,0:T(8,128)}, f32[8,512]{1,0:T(8,128)}, f32[32,512]{1,0:T(8,128)}) custom-call(bf16[512,512]{1,0:T(8,128)(2,1)} %bitcast.3, bf16[512,128]{1,0:T(8,128)(2,1)} %bitcast.4, s32[8,512]{1,0:T(8,128)} %neigh_ref.1, s32[1]{0:T(128)S(6)} %copy.15.region_ref, ...), custom_call_target="tpu_custom_call" | custom-call | tf_op jit(solution)/shard_map/pallas_call | solution.py:526
  41.6 22.7 %shard_map.138 = (bf16[512,512]{1,0:T(8,128)(2,1)}, f32[32,512]{1,0:T(8,128)}, f32[8,512]{1,0:T(8,128)}, f32[32,512]{1,0:T(8,128)}, f32[8]{0:T(128)}) custom-call(bf16[512,512]{1,0:T(8,128)(2,1)} %get-tuple-element.15.refs_0_, f32[32,512]{1,0:T(8,128)} %get-tuple-element.16.refs_1_, f32[8,512]{1,0:T(8,128)} %get-tuple-element.17.refs_2_, ...), custom_call_target="tpu_custom_call" | custom-call | tf_op jit(solution)/shard_map/pallas_call | solution.py:541

commit v3 on v2

--- a/solution.py
+++ b/solution.py
@@ -41,8 +41,8 @@
 def orders(tiles):
     digits = tile_digits(tiles)
     first = [digits[0], "member"] + digits[1:]
-    second = digits[:2] + ["member"] + digits[2:]
-    third = digits[:1] + digits[2:] + ["member"] + digits[1:2]
+    second = digits
+    third = digits[:1] + digits[2:] + digits[1:2]
     return first, second, third
 
 
@@ -281,6 +281,7 @@
         sent["noise", o].wait_recv()
         student(o)
     chunk = 16
+    lanes = 256 if width % 256 == 0 else width
     scale = 1.0 / math.sqrt(cells * tiles)
     c_cross = 1.0 / (members * members)
     c_within = 1.0 / (members * (members - 1))
@@ -288,38 +289,41 @@
     def visit(i, losses):
         base = pl.multiple_of(i * chunk, chunk)
         rows = [pl.ds(pl.multiple_of(j * block + base, chunk), chunk) for j in range(members)]
-        st = [s_all[r, :].astype(F32) for r in rows]
-        te = [t_all[r, :].astype(F32) for r in rows]
-        grads = [jnp.zeros((chunk, width), F32) for _ in rows]
-        cross = jnp.zeros((chunk, width), F32)
-        within = jnp.zeros((chunk, width), F32)
-        for a in range(members):
-            for b in range(members):
-                d = st[a] - te[b]
-                q = d * d + 0.01
-                inv = lax.rsqrt(q)
-                grads[a] = grads[a] + d * inv
-                cross = cross + (q * inv - 0.1)
-        grads = [g * c_cross for g in grads]
-        for a in range(members):
-            for b in range(a + 1, members):
-                d = st[a] - st[b]
-                q = d * d + 0.01
-                inv = lax.rsqrt(q)
-                slope = d * inv * c_within
-                grads[a] = grads[a] - slope
-                grads[b] = grads[b] + slope
-                within = within + (q * inv - 0.1)
-        for r, g in zip(rows, grads):
-            g_all[r, :] = (g * scale).astype(BF16)
-        return losses + (cross * c_cross - within * c_within)
+        for at in range(0, width, lanes):
+            cols = pl.ds(at, lanes)
+            st = [s_all[r, cols].astype(F32) for r in rows]
+            te = [t_all[r, cols].astype(F32) for r in rows]
+            grads = [jnp.zeros((chunk, lanes), F32) for _ in rows]
+            cross = jnp.zeros((chunk, lanes), F32)
+            within = jnp.zeros((chunk, lanes), F32)
+            for a in range(members):
+                for b in range(members):
+                    d = st[a] - te[b]
+                    q = d * d + 0.01
+                    inv = lax.rsqrt(q)
+                    grads[a] = grads[a] + d * inv
+                    cross = cross + (q * inv - 0.1)
+            grads = [g * c_cross for g in grads]
+            for a in range(members):
+                for b in range(a + 1, members):
+                    d = st[a] - st[b]
+                    q = d * d + 0.01
+                    inv = lax.rsqrt(q)
+                    slope = d * inv * c_within
+                    grads[a] = grads[a] - slope
+                    grads[b] = grads[b] + slope
+                    within = within + (q * inv - 0.1)
+            for r, g in zip(rows, grads):
+                g_all[r, cols] = (g * scale).astype(BF16)
+            losses = losses + (cross * c_cross - within * c_within)
+        return losses
 
     def backward(c):
         for j in range(members):
             rows = pl.ds(j * block + c * part_rows, part_rows)
             gpre_all[rows, :] = (dot_nt(g_all[rows, :], sout_ref[...]) * slope_all[rows, :]).astype(BF16)
 
-    losses = jnp.zeros((chunk, width), F32)
+    losses = jnp.zeros((chunk, lanes), F32)
     steps = part_rows // chunk
     for c in range(parts):
         for o in range(1, members):
@@ -329,7 +333,7 @@
             backward(c)
     total = jnp.sum(losses, keepdims=True)
     lane = lax.broadcasted_iota(jnp.int32, (8, 128), 1)
-    onehot = jnp.where(lane == region_ref[0], 1.0, 0.0) * total
+    onehot = jnp.where(lane == region_ref[...], 1.0, 0.0) * total
 
     if not reduce_here:
         loss_ref[...] = onehot
@@ -347,8 +351,7 @@
             wire.append([bufs.pop(0) for _ in order])
             part.append([bufs.pop(0) for _ in order])
             land.append([bufs.pop(0) for _ in order])
-            final = bufs.pop(0)
-            share.append((final, bufs.pop(0)))
+            share.append(bufs.pop(0))
         column = width // members
         loss_now = [onehot]
 
@@ -382,7 +385,7 @@
                     part[s][k + 1][i] = value
                     wire[s][k + 1][i] = value.astype(BF16)
                 else:
-                    share[s][0][...] = value.astype(BF16)
+                    share[s][m] = value.astype(BF16)
 
         def start_loss(k):
             step = streams[0][k]
@@ -405,12 +408,13 @@
 
         def put(s, acc):
             rows = acc.shape[0] // tiles
-            for i in range(members):
+            span = column if "member" in streams[s] else width
+            for i in range(width // span):
                 for j in range(tiles):
                     slot = slot_of(streams[s], members, i, j)
-                    value = acc[j * rows : (j + 1) * rows, i * column : (i + 1) * column]
+                    value = acc[j * rows : (j + 1) * rows, i * span : (i + 1) * span]
                     if rows % 16:
-                        value = jnp.concatenate([value, jnp.zeros((-rows % 16, column), F32)])
+                        value = jnp.concatenate([value[:, : span // 2], value[:, span // 2 :]])
                     part[s][0][slot] = value
                     wire[s][0][slot] = value.astype(BF16)
 
@@ -420,35 +424,47 @@
         backward(parts - 1)
         put(1, dot_tn(x_all[...], gpre_all[...]))
         start(1, 0)
+        finish(0, 0)
+        start(0, 1)
         put(2, dot_tn(n_all[...], gpre_all[...]))
         start(2, 0)
-        last = len(streams[0])
-        for k in range(last):
+
+        def start_share(s):
+            for o in range(1, members):
+                device, _ = peer("member", o)
+                c = copy(("share", s, o), share[s].at[m], share[s].at[m], device)
+                c.start()
+                sent["share", s, o] = c
+
+        for k in range(len(streams[0])):
             finish_loss(k)
-            if k + 1 < last:
+            if k + 1 < len(streams[0]):
                 start_loss(k + 1)
             for s in range(len(streams)):
-                finish(s, k)
-                if k + 1 < last:
-                    start(s, k + 1)
-                else:
-                    for o in range(1, members):
-                        device, _ = peer("member", o)
-                        c = copy(("share", s, o), share[s][0], share[s][1].at[o - 1], device)
-                        c.start()
-                        sent["share", s, o] = c
+                if k < len(streams[s]):
+                    if (s, k) != (0, 0):
+                        finish(s, k)
+                        if k + 1 < len(streams[s]):
+                            start(s, k + 1)
+                        else:
+                            start_share(s)
         loss_ref[...] = loss_now[0] * (1.0 / (cells * tiles // REGIONS * width))
-
-        def emit(s, value, member):
-            cols = pl.ds(pl.multiple_of(member * column, column), column)
-            out = (gout_ref, gin_ref, gnoise_ref)[s]
-            out[:, cols] = value[: out.shape[0]]
-
-        for s in range(len(streams)):
-            emit(s, share[s][0][...].astype(F32), m)
+        for s in (1, 2, 0):
             for o in range(1, members):
                 sent["share", s, o].wait_recv()
-                emit(s, share[s][1][o - 1].astype(F32), lax.rem(m + members - o, members))
+            pieces = [share[s][j].astype(F32) for j in range(members)]
+            if s == 0:
+                for j in range(members):
+                    gout_ref[:, j * column : (j + 1) * column] = pieces[j]
+            else:
+                total = sum(pieces[1:], pieces[0])
+                if s == 1:
+                    gin_ref[...] = total
+                else:
+                    rows = gnoise_ref.shape[0]
+                    if rows % 16:
+                        total = jnp.concatenate([total[:rows], total[rows:]], axis=1)
+                    gnoise_ref[...] = total
         for c in sent.values():
             c.wait_send()
 
@@ -462,13 +478,9 @@
 
 
 def hand_on(*refs):
-    loss_ref, region_ref, sem = refs[4], refs[9], refs[10]
-    copies = [pltpu.make_async_copy(refs[i], refs[5 + i], sem.at[i]) for i in range(4)]
-    for c in copies:
-        c.start()
-    region_ref[...] = loss_ref[0, : region_ref.shape[0]]
-    for c in copies:
-        c.wait()
+    for i in range(4):
+        refs[5 + i][...] = refs[i][...]
+    refs[9][...] = refs[4][0, : refs[9].shape[0]]
 
 
 def on_device(members, tiles, *args):
@@ -508,18 +520,18 @@
         streams = orders(tiles)
         for step in streams[0]:
             scratch.append(pltpu.VMEM((count_of(step, members), 8, 128), F32))
-        high = [rows[0], rows[1], -(-rows[2] // 16) * 16]
-        for order, tall in zip(streams, high):
+        noise_piece = (2 * rows[2], width // 2) if rows[2] % 16 else (rows[2], width)
+        pieces = [(rows[0], column), (rows[1], width), noise_piece]
+        for order, piece in zip(streams, pieces):
             sizes = []
-            left = members * tiles
+            left = (members if "member" in order else 1) * tiles
             for step in order:
                 sizes.append((left, count_of(step, members)))
                 left //= count_of(step, members)
-            scratch += [pltpu.VMEM((size, tall, column), BF16) for size, _ in sizes]
-            scratch += [pltpu.VMEM((size, tall, column), F32) for size, _ in sizes]
-            scratch += [pltpu.VMEM((n - 1, size // n, tall, column), BF16) for size, n in sizes]
-            scratch.append(pltpu.VMEM((tall, column), BF16))
-            scratch.append(pltpu.VMEM((members - 1, tall, column), BF16))
+            scratch += [pltpu.VMEM((size,) + piece, BF16) for size, _ in sizes]
+            scratch += [pltpu.VMEM((size,) + piece, F32) for size, _ in sizes]
+            scratch += [pltpu.VMEM((n - 1, size // n) + piece, BF16) for size, n in sizes]
+            scratch.append(pltpu.VMEM((members,) + piece, BF16))
     else:
         shapes = ((width, hidden), (draws, hidden), (hidden, width))
     vmem = pl.BlockSpec(memory_space=pltpu.VMEM)
@@ -527,24 +539,22 @@
         functools.partial(kernel, members, tiles, reduce_here),
         out_shape=[jax.ShapeDtypeStruct((cells, width), BF16), jax.ShapeDtypeStruct((8, 128), F32)]
         + [jax.ShapeDtypeStruct(s, F32) for s in shapes],
-        in_specs=[vmem] * 3 + [pl.BlockSpec(memory_space=pltpu.SMEM)]
+        in_specs=[vmem] * 3 + [vmem]
         + [pl.BlockSpec(memory_space=pl.ANY)] * 6,
         out_specs=[vmem] * 5,
         scratch_shapes=scratch,
         compiler_params=pltpu.CompilerParams(
             collective_id=0, has_side_effects=True, vmem_limit_bytes=56 * 1024 * 1024
         ),
-    )(state, noise, neighbours, region_map, *weights)
+    )(state, noise, neighbours, region_map.reshape(1, 1), *weights)
     if reduce_here:
-        hbm = pl.BlockSpec(memory_space=pl.ANY)
         big = (teacher, gin, gnoise, gout)
         teacher, gin, gnoise, gout, region_loss = pl.pallas_call(
             hand_on,
             out_shape=[jax.ShapeDtypeStruct(a.shape, a.dtype) for a in big]
             + [jax.ShapeDtypeStruct((REGIONS,), F32)],
-            in_specs=[hbm] * 4 + [vmem],
-            out_specs=[hbm] * 4 + [vmem],
-            scratch_shapes=[pltpu.SemaphoreType.DMA((4,))],
+            in_specs=[vmem] * 5,
+            out_specs=[vmem] * 5,
         )(*big, loss)
     else:
         region_loss = loss[0, :REGIONS]

time: 64.4 us -> 43 us (0.67)
  Pallas kernels: 63 us -> 41.5 us
    pallas_call x1, Pallas kernels: 22.7 us -> 1.97 us  [on_device(): pl.pallas_call(hand_on, out_shape=[jax.ShapeDtypeStruct(a.shape, a.dtype)...]
    pallas_call x1, Pallas kernels: 40.3 us -> 39.5 us  [on_device(): pl.pallas_call(functools.partial(kernel, members, tiles, reduce_here), ou...]
where the time goes in v3:
time: 43 us; the launch traced here: 42.8 us
  Pallas kernels  41.5 us (97%)
  between operations  1.29 us (3%)
    pallas_call x1, Pallas kernels, on_device(): pl.pallas_call(functools.partial(kernel, members, tiles, reduce_here), ou...  39.5 us
    pallas_call x1, Pallas kernels, on_device(): pl.pallas_call(hand_on, out_shape=[jax.ShapeDtypeStruct(a.shape, a.dtype)...  1.97 us

profile of v3, /device:TPU:0, one launch (start us, length us, event | category | flops | bytes accessed | tf_op | source)
XLA Modules:
  0.0 42.8 jit_solution(16086313069724402777)
XLA Ops:
  1.3 39.5 %shard_map.137 = (bf16[512,512]{1,0:T(8,128)(2,1)}, f32[8,128]{1,0:T(8,128)}, f32[32,512]{1,0:T(8,128)}, f32[8,512]{1,0:T(8,128)}, f32[32,512]{1,0:T(8,128)}) custom-call(bf16[512,512]{1,0:T(8,128)(2,1)} %bitcast.5, bf16[512,128]{1,0:T(8,128)(2,1)} %bitcast.6, s32[8,512]{1,0:T(8,128)} %neigh_ref.1, s32[1,1]{1,0:T(1,128)} %bitcast.4.region_ref, ...), custom_call_target="tpu_custom_call" | custom-call | tf_op jit(solution)/shard_map/pallas_call | solution.py:538
  40.8 2.0 %shard_map.138 = (bf16[512,512]{1,0:T(8,128)(2,1)}, f32[32,512]{1,0:T(8,128)}, f32[8,512]{1,0:T(8,128)}, f32[32,512]{1,0:T(8,128)}, f32[8]{0:T(128)}) custom-call(bf16[512,512]{1,0:T(8,128)(2,1)} %get-tuple-element.15.refs_0_, f32[32,512]{1,0:T(8,128)} %get-tuple-element.16.refs_1_, f32[8,512]{1,0:T(8,128)} %get-tuple-element.17.refs_2_, ...), custom_call_target="tpu_custom_call" | custom-call | tf_op jit(solution)/shard_map/pallas_call | solution.py:552

commit v4 on v3

--- a/solution.py
+++ b/solution.py
@@ -21,10 +21,6 @@
 
 def dot_tn(a, b):
     return lax.dot_general(a, b, (((0,), (0,)), ((), ())), preferred_element_type=F32)
-
-
-def dot_nt(a, b):
-    return lax.dot_general(a, b, (((1,), (1,)), ((), ())), preferred_element_type=F32)
 
 
 def tile_digits(tiles):
@@ -59,7 +55,7 @@
 
 
 def parts_of(block):
-    return 2 if block % 32 == 0 else 1
+    return 4 if block % 64 == 0 else 1
 
 
 def layout(members, tiles, parts):
@@ -81,17 +77,17 @@
     members,
     tiles,
     reduce_here,
-    state_ref,
-    noise_ref,
-    neigh_ref,
-    region_ref,
+    state_hbm,
+    noise_hbm,
+    neigh_hbm,
+    region_hbm,
     msg_hbm,
     up_hbm,
     down_hbm,
     sin_hbm,
     snoise_hbm,
     sout_hbm,
-    teacher_ref,
+    teacher_hbm,
     loss_ref,
     gin_ref,
     gnoise_ref,
@@ -106,6 +102,13 @@
     sh_all,
     g_all,
     gpre_all,
+    x_turned,
+    n_turned,
+    sh_turned,
+    sout_turned,
+    teacher_ref,
+    neigh_ref,
+    region_ref,
     msg_ref,
     up_ref,
     down_ref,
@@ -117,7 +120,7 @@
     recv_sem,
     *bufs,
 ):
-    cells, width = state_ref.shape
+    cells, width = state_hbm.shape
     block = cells // members
     m = lax.axis_index("member")
     t = lax.axis_index("tile")
@@ -149,18 +152,20 @@
             device_id_type=MESH,
         )
 
+    own = pl.ds(pl.multiple_of(m * block, block), block)
     pairs = [
+        (state_hbm.at[own], x_all.at[pl.ds(0, block)]),
+        (noise_hbm.at[own], n_all.at[pl.ds(0, block)]),
         (sin_hbm, sin_ref),
         (snoise_hbm, snoise_ref),
         (sout_hbm, sout_ref),
+        (state_hbm, ext.at[pl.ds(HALO, cells)]),
+        (neigh_hbm, neigh_ref),
         (msg_hbm, msg_ref),
         (up_hbm, up_ref),
         (down_hbm, down_ref),
+        (region_hbm, region_ref),
     ]
-    loads = [pltpu.make_async_copy(a, b, load_sem.at[i]) for i, (a, b) in enumerate(pairs)]
-    for load in loads:
-        load.start()
-
     barrier = pltpu.get_barrier_semaphore()
     groups = ["member"] + (tile_digits(tiles) if reduce_here else [])
     waits = 0
@@ -178,11 +183,14 @@
     def _():
         pl.semaphore_signal(barrier, inc=1, device_id=(m, t + 1), device_id_type=MESH)
 
+    loads = [pltpu.make_async_copy(a, b, load_sem.at[i]) for i, (a, b) in enumerate(pairs)]
+    for load in loads:
+        load.start()
     ends = jnp.where(t > 0, 1, 0) + jnp.where(t < tiles - 1, 1, 0)
     pl.semaphore_wait(barrier, waits + ends)
 
-    to_left = copy("left", state_ref.at[pl.ds(0, HALO)], ext.at[pl.ds(HALO + cells, HALO)], (m, t - 1))
-    to_right = copy("right", state_ref.at[pl.ds(cells - HALO, HALO)], ext.at[pl.ds(0, HALO)], (m, t + 1))
+    to_left = copy("left", state_hbm.at[pl.ds(0, HALO)], ext.at[pl.ds(HALO + cells, HALO)], (m, t - 1))
+    to_right = copy("right", state_hbm.at[pl.ds(cells - HALO, HALO)], ext.at[pl.ds(0, HALO)], (m, t + 1))
 
     @pl.when(t > 0)
     def _():
@@ -198,8 +206,8 @@
         device, other = peer("member", o)
         rows = pl.ds(pl.multiple_of(other * block, block), block)
         slot = pl.ds(o * block, block)
-        sent["state", o] = copy(("state", o), state_ref.at[rows], x_all.at[slot], device)
-        sent["noise", o] = copy(("noise", o), noise_ref.at[rows], n_all.at[slot], device)
+        sent["state", o] = copy(("state", o), state_hbm.at[rows], x_all.at[slot], device)
+        sent["noise", o] = copy(("noise", o), noise_hbm.at[rows], n_all.at[slot], device)
         sent["state", o].start()
         sent["noise", o].start()
         for c in range(parts):
@@ -207,11 +215,6 @@
             slot = pl.ds(o * block + c * part_rows, part_rows)
             name = ("teacher", o, c)
             sent[name] = copy(name, teacher_ref.at[rows], t_all.at[slot], device)
-
-    own = pl.ds(pl.multiple_of(m * block, block), block)
-    x_all[pl.ds(0, block)] = state_ref[own, :]
-    n_all[pl.ds(0, block)] = noise_ref[own, :]
-    ext[pl.ds(HALO, cells)] = state_ref[...]
 
     def student(o):
         rows = pl.ds(o * block, block)
@@ -223,7 +226,7 @@
         sh_all[rows, :] = sh
         s_all[rows, :] = (x.astype(F32) + dot(sh, sout_ref[...])).astype(BF16)
 
-    for load in loads[:3]:
+    for load in loads[:5]:
         load.wait()
     student(0)
 
@@ -244,6 +247,9 @@
     @pl.when(t == tiles - 1)
     def _():
         ext[pl.ds(HALO + cells, HALO)] = zeros
+
+    for load in loads[5:]:
+        load.wait()
 
     span = 128
     reach = span + 2 * HALO
@@ -257,8 +263,9 @@
         total = dot_tn(times.astype(BF16), ext[pl.ds(b * span, reach), :])
         gathered[pl.ds(b * span, span)] = (total / nbrs).astype(BF16)
 
-    def teacher(rows):
-        resid = state_ref[rows, :].astype(F32) + dot(gathered[rows, :], msg_ref[...])
+    def teacher(at):
+        rows = pl.ds(at, block)
+        resid = ext[pl.ds(at + HALO, block), :].astype(F32) + dot(gathered[rows, :], msg_ref[...])
         mean = jnp.mean(resid * resid, axis=1, keepdims=True)
         normed = (resid * lax.rsqrt(mean + 1e-06)).astype(BF16)
         up = dot(normed, up_ref[...])
@@ -267,19 +274,23 @@
         teacher_ref[rows, :] = out
         return out
 
-    for load in loads[3:]:
-        load.wait()
     for o in range(1, members):
         _, other = peer("member", o)
-        teacher(pl.ds(pl.multiple_of(other * block, block), block))
+        teacher(pl.multiple_of(other * block, block))
         for c in range(parts):
             sent["teacher", o, c].start()
-    t_all[pl.ds(0, block)] = teacher(own)
+    t_all[pl.ds(0, block)] = teacher(pl.multiple_of(m * block, block))
+    result = pltpu.make_async_copy(teacher_ref, teacher_hbm, load_sem.at[len(pairs)])
+    result.start()
 
     for o in range(1, members):
         sent["state", o].wait_recv()
         sent["noise", o].wait_recv()
         student(o)
+    x_turned[...] = x_all[...].T
+    n_turned[...] = n_all[...].T
+    sh_turned[...] = sh_all[...].T
+    sout_turned[...] = sout_ref[...].T
     chunk = 16
     lanes = 256 if width % 256 == 0 else width
     scale = 1.0 / math.sqrt(cells * tiles)
@@ -319,9 +330,11 @@
         return losses
 
     def backward(c):
-        for j in range(members):
-            rows = pl.ds(j * block + c * part_rows, part_rows)
-            gpre_all[rows, :] = (dot_nt(g_all[rows, :], sout_ref[...]) * slope_all[rows, :]).astype(BF16)
+        rows = [pl.ds(j * block + c * part_rows, part_rows) for j in range(members)]
+        grads = dot(jnp.concatenate([g_all[r, :] for r in rows]), sout_turned[...])
+        for j, r in enumerate(rows):
+            g = grads[j * part_rows : (j + 1) * part_rows]
+            gpre_all[r, :] = (g * slope_all[r, :]).astype(BF16)
 
     losses = jnp.zeros((chunk, lanes), F32)
     steps = part_rows // chunk
@@ -337,10 +350,10 @@
 
     if not reduce_here:
         loss_ref[...] = onehot
-        gout_ref[...] = dot_tn(sh_all[...], g_all[...])
+        gout_ref[...] = dot(sh_turned[...], g_all[...])
         backward(parts - 1)
-        gin_ref[...] = dot_tn(x_all[...], gpre_all[...])
-        gnoise_ref[...] = dot_tn(n_all[...], gpre_all[...])
+        gin_ref[...] = dot(x_turned[...], gpre_all[...])
+        gnoise_ref[...] = dot(n_turned[...], gpre_all[...])
         for c in sent.values():
             c.wait_send()
     else:
@@ -419,14 +432,14 @@
                     wire[s][0][slot] = value.astype(BF16)
 
         start_loss(0)
-        put(0, dot_tn(sh_all[...], g_all[...]))
+        put(0, dot(sh_turned[...], g_all[...]))
         start(0, 0)
         backward(parts - 1)
-        put(1, dot_tn(x_all[...], gpre_all[...]))
+        put(1, dot(x_turned[...], gpre_all[...]))
         start(1, 0)
         finish(0, 0)
         start(0, 1)
-        put(2, dot_tn(n_all[...], gpre_all[...]))
+        put(2, dot(n_turned[...], gpre_all[...]))
         start(2, 0)
 
         def start_share(s):
@@ -468,6 +481,8 @@
         for c in sent.values():
             c.wait_send()
 
+    result.wait()
+
     @pl.when(t > 0)
     def _():
         to_left.wait_send()
@@ -511,10 +526,17 @@
         pltpu.VMEM((cells, hidden), BF16),
         pltpu.VMEM((cells, width), BF16),
         pltpu.VMEM((cells, hidden), BF16),
+        pltpu.VMEM((width, cells), BF16),
+        pltpu.VMEM((draws, cells), BF16),
+        pltpu.VMEM((hidden, cells), BF16),
+        pltpu.VMEM((width, hidden), BF16),
+        pltpu.VMEM((cells, width), BF16),
+        pltpu.VMEM(neighbours.shape, neighbours.dtype),
+        pltpu.VMEM((1, 1), region_map.dtype),
     ]
     scratch += [pltpu.VMEM(w.shape, w.dtype) for w in weights]
     copies = len(layout(members, tiles, parts_of(cells // members)))
-    scratch += [pltpu.SemaphoreType.DMA((n,)) for n in (len(weights), copies, copies)]
+    scratch += [pltpu.SemaphoreType.DMA((n,)) for n in (len(weights) + 6, copies, copies)]
     if reduce_here:
         shapes = ((rows[1], width), (rows[2], width), (rows[0], width))
         streams = orders(tiles)
@@ -539,9 +561,8 @@
         functools.partial(kernel, members, tiles, reduce_here),
         out_shape=[jax.ShapeDtypeStruct((cells, width), BF16), jax.ShapeDtypeStruct((8, 128), F32)]
         + [jax.ShapeDtypeStruct(s, F32) for s in shapes],
-        in_specs=[vmem] * 3 + [vmem]
-        + [pl.BlockSpec(memory_space=pl.ANY)] * 6,
-        out_specs=[vmem] * 5,
+        in_specs=[pl.BlockSpec(memory_space=pl.ANY)] * 10,
+        out_specs=[pl.BlockSpec(memory_space=pl.ANY)] + [vmem] * 4,
         scratch_shapes=scratch,
         compiler_params=pltpu.CompilerParams(
             collective_id=0, has_side_effects=True, vmem_limit_bytes=56 * 1024 * 1024

time: 43 us -> 41.3 us (0.960)
  Pallas kernels: 41.5 us -> 39.9 us
    pallas_call x1, Pallas kernels: 39.5 us -> 37.9 us  [on_device(): pl.pallas_call(functools.partial(kernel, members, tiles, reduce_here), ou...]
where the time goes in v4:
time: 41.3 us; the launch traced here: 41.2 us
  Pallas kernels  39.9 us (97%)
  between operations  1.29 us (3%)
    pallas_call x1, Pallas kernels, on_device(): pl.pallas_call(functools.partial(kernel, members, tiles, reduce_here), ou...  37.9 us
    pallas_call x1, Pallas kernels, on_device(): pl.pallas_call(hand_on, out_shape=[jax.ShapeDtypeStruct(a.shape, a.dtype)...  1.97 us

profile of v4, /device:TPU:0, one launch (start us, length us, event | category | flops | bytes accessed | tf_op | source)
XLA Modules:
  0.0 41.2 jit_solution(11207315431845931927)
XLA Ops:
  1.3 37.9 %shard_map.137 = (bf16[512,512]{1,0:T(8,128)(2,1)}, f32[8,128]{1,0:T(8,128)}, f32[32,512]{1,0:T(8,128)}, f32[8,512]{1,0:T(8,128)}, f32[32,512]{1,0:T(8,128)}) custom-call(bf16[512,512]{1,0:T(8,128)(2,1)} %bitcast.5, bf16[512,128]{1,0:T(8,128)(2,1)} %bitcast.6, s32[8,512]{1,0:T(8,128)} %neigh_hbm.1, s32[1,1]{1,0:T(1,128)} %bitcast.4.region_hbm, ...), custom_call_target="tpu_custom_call" | custom-call | tf_op jit(solution)/shard_map/pallas_call | solution.py:560
  39.2 2.0 %shard_map.138 = (bf16[512,512]{1,0:T(8,128)(2,1)}, f32[32,512]{1,0:T(8,128)}, f32[8,512]{1,0:T(8,128)}, f32[32,512]{1,0:T(8,128)}, f32[8]{0:T(128)}) custom-call(bf16[512,512]{1,0:T(8,128)(2,1)} %get-tuple-element.15.refs_0_, f32[32,512]{1,0:T(8,128)} %get-tuple-element.16.refs_1_, f32[8,512]{1,0:T(8,128)} %get-tuple-element.17.refs_2_, ...), custom_call_target="tpu_custom_call" | custom-call | tf_op jit(solution)/shard_map/pallas_call | solution.py:573

commit v5 on v4

--- a/solution.py
+++ b/solution.py
@@ -435,10 +435,11 @@
         put(0, dot(sh_turned[...], g_all[...]))
         start(0, 0)
         backward(parts - 1)
-        put(1, dot(x_turned[...], gpre_all[...]))
-        start(1, 0)
+        acc_in = dot(x_turned[...], gpre_all[...])
         finish(0, 0)
         start(0, 1)
+        put(1, acc_in)
+        start(1, 0)
         put(2, dot(n_turned[...], gpre_all[...]))
         start(2, 0)
 

time: 41.3 us -> 41.6 us (level)
  no operation moved by 1% of the time
where the time goes in v5:
time: 41.6 us; the launch traced here: 41.4 us
  Pallas kernels  40.1 us (96%)
  between operations  1.29 us (3%)
    pallas_call x1, Pallas kernels, on_device(): pl.pallas_call(functools.partial(kernel, members, tiles, reduce_here), ou...  38.2 us
    pallas_call x1, Pallas kernels, on_device(): pl.pallas_call(hand_on, out_shape=[jax.ShapeDtypeStruct(a.shape, a.dtype)...  1.97 us

profile of v5, /device:TPU:0, one launch (start us, length us, event | category | flops | bytes accessed | tf_op | source)
XLA Modules:
  0.0 41.4 jit_solution(14588321199754273261)
XLA Ops:
  1.3 38.2 %shard_map.137 = (bf16[512,512]{1,0:T(8,128)(2,1)}, f32[8,128]{1,0:T(8,128)}, f32[32,512]{1,0:T(8,128)}, f32[8,512]{1,0:T(8,128)}, f32[32,512]{1,0:T(8,128)}) custom-call(bf16[512,512]{1,0:T(8,128)(2,1)} %bitcast.5, bf16[512,128]{1,0:T(8,128)(2,1)} %bitcast.6, s32[8,512]{1,0:T(8,128)} %neigh_hbm.1, s32[1,1]{1,0:T(1,128)} %bitcast.4.region_hbm, ...), custom_call_target="tpu_custom_call" | custom-call | tf_op jit(solution)/shard_map/pallas_call | solution.py:561
  39.4 2.0 %shard_map.138 = (bf16[512,512]{1,0:T(8,128)(2,1)}, f32[32,512]{1,0:T(8,128)}, f32[8,512]{1,0:T(8,128)}, f32[32,512]{1,0:T(8,128)}, f32[8]{0:T(128)}) custom-call(bf16[512,512]{1,0:T(8,128)(2,1)} %get-tuple-element.15.refs_0_, f32[32,512]{1,0:T(8,128)} %get-tuple-element.16.refs_1_, f32[8,512]{1,0:T(8,128)} %get-tuple-element.17.refs_2_, ...), custom_call_target="tpu_custom_call" | custom-call | tf_op jit(solution)/shard_map/pallas_call | solution.py:574
